TPU v7x, 32 devices: a whole 2x2x4 slice. The times are simulated.
32 devices in a mesh: grp: 2 (over y), leaf: 4 (over z), vec: 2 (over x), sub: 2 (over core).
Axes of the slice: x: 2, y: 2, z: 4, core: 2. Of those that a mesh axis runs over, the one named last changes fastest.
Arguments:
- vectors: bfloat16 [128, 32768], P(('grp', 'vec'), ('leaf', 'sub')), parts along dimension 0, may hold values from -6 to 6
- coords: bfloat16 [6, 32768], P('grp', ('leaf', 'sub')), parts along dimension 0, may hold values from 0 to 1
- point_order: int32 [65536], P(('grp', 'leaf', 'sub')), parts along dimension 0, may hold values from 0 to 32767, as said below
- leaf_basis: bfloat16 [256, 64, 256], P(('grp', 'leaf', 'sub')), parts along dimension 0, may hold values from -0.375 to 0.375
- transfer_local: bfloat16 [480, 4096], P(('grp', 'leaf', 'sub')), parts along dimension 0, may hold values from -0.5 to 0.5
- transfer_top: bfloat16 [24, 4096], P('grp'), parts along dimension 0, may hold values from -0.5 to 0.5
- partners_local: int32 [496, 4], P(('grp', 'leaf', 'sub')), parts along dimension 0, may hold values from 0 to 247, as said below
- coupling_local: bfloat16 [496, 4, 4096], P(('grp', 'leaf', 'sub')), parts along dimension 0, may hold values from -1 to 1
- top_partners: int32 [12, 2], P('grp'), parts along dimension 0, may hold values from 0 to 3, as said below
- top_coupling: bfloat16 [12, 2, 4096], P('grp'), parts along dimension 0, may hold values from -2.828427 to 2.828427
Outputs:
- product: bfloat16 [128, 32768], P(('grp', 'vec'), ('leaf', 'sub')), parts along dimension 0
There are 2 independent parts, one for each index of `grp`. A program takes and returns all parts, laid end to end along the dimension named above; each array names one. Nothing has to cross between parts.
Inputs may be any that keep to these rules, and one draw needn't show every extreme that they name: `point_order`: A permutation of the positions. Of the 4096 points in one aligned block of the input order, at most 1408 go to one subtree's block of positions, and one subtree receives exactly 1408 from one block in every draw. `partners_local`: each entry is a row number as in the steps of a node on the same level as the row's own node, in the same subtree or in the one just before or after it, never the node itself. `top_partners`: each entry is another node of the same top level.
All inputs are finite; a program needn't handle non-finite values.
Results may differ from a plain program's by a relative error of at most 0.011.
Values may be sent and summed in bfloat16 or wider, within the bound.
A program may use at most 64 MiB of HBM per device.

v0:
```python
import functools

import jax
import jax.numpy as jnp
from jax import lax
from jax.experimental import pallas as pl
from jax.experimental.pallas import tpu as pltpu
from jax.sharding import PartitionSpec as P

ROOT_THREE = 1.7320508075688772
LENGTH_SCALE = 0.0125
KERNEL_GAIN = 0.25
LOG2_E = 1.4426950408889634
MESH = pl.DeviceIdType.MESH
VMEM_LIMIT = 56 * 1024 * 1024
CHUNK = 1024
FIELDS = 8


def for_each_block(lines, pairs, sems, process):
    send_sem, pass_sem, recv_sem = sems
    mine = lax.axis_index("leaf")
    core = lax.axis_index("sub")
    other = 1 - core
    me = mine * 2 + core
    barrier = pltpu.get_barrier_semaphore()
    for hop in range(1, lines):
        target = lax.rem(mine + hop, lines)
        pl.semaphore_signal(barrier, inc=1, device_id={"leaf": target}, device_id_type=MESH)
    pl.semaphore_signal(barrier, inc=1, device_id={"sub": other}, device_id_type=MESH)
    pl.semaphore_wait(barrier, lines)

    def sends(hop):
        target = lax.rem(mine + hop, lines)
        return [
            pltpu.make_async_remote_copy(
                src_ref=own,
                dst_ref=held.at[me],
                send_sem=send_sem.at[which, hop],
                recv_sem=recv_sem.at[which, me],
                device_id={"leaf": target},
                device_id_type=MESH,
            )
            for which, (own, held) in enumerate(pairs)
        ]

    def across(hop, block):
        return [
            pltpu.make_async_remote_copy(
                src_ref=held.at[block],
                dst_ref=held.at[block],
                send_sem=pass_sem.at[which, hop],
                recv_sem=recv_sem.at[which, block],
                device_id={"sub": other},
                device_id_type=MESH,
            )
            for which, (own, held) in enumerate(pairs)
        ]

    def begin(hop, carry):
        for copy in sends(hop):
            copy.start()
        return carry

    lax.fori_loop(1, lines, begin, 0)
    for own, held in pairs:
        held[me] = own[...]

    def step(hop, carry):
        line = lax.rem(mine + lines - hop, lines)
        near_block = line * 2 + core
        far_block = line * 2 + other

        @pl.when(hop > 0)
        def _():
            for copy in across(hop, near_block):
                copy.wait_recv()

        for copy in across(hop, near_block):
            copy.start()
        process(near_block)
        for copy in across(hop, far_block):
            copy.wait_recv()
        process(far_block)
        return carry

    lax.fori_loop(0, lines, step, 0)

    def finish(hop, carry):
        for copy in sends(hop):
            copy.wait_send()
        return carry

    lax.fori_loop(1, lines, finish, 0)

    def finish_across(hop, carry):
        for copy in across(hop, lax.rem(mine + lines - hop, lines) * 2 + core):
            copy.wait_send()
        return carry

    lax.fori_loop(0, lines, finish_across, 0)


def arrange_kernel(
    lines, leaves, x_ref, aux_ref, v_out, c_out, x_all, aux_all, total, send_sem, pass_sem, recv_sem
):
    me = lax.axis_index("leaf") * 2 + lax.axis_index("sub")
    rows = x_ref.shape[0]
    dev_pts = x_ref.shape[1]
    leaf_pts = v_out.shape[1]
    slots = leaves + 2
    slot_pad = -(-slots // 8) * 8
    total[...] = jnp.zeros_like(total)

    def process(block):
        aux = aux_all[block].astype(jnp.float32)
        for part in range(dev_pts // CHUNK):
            fields = aux[part * FIELDS : (part + 1) * FIELDS]
            x = x_all[block, :, part * CHUNK : (part + 1) * CHUNK]
            slot = (fields[5:6] - me.astype(jnp.float32)) * leaves + fields[4:5] + 1.0
            slot_here = jnp.broadcast_to(slot, (rows, CHUNK)).astype(jnp.int32)
            zero = jnp.zeros_like(x)
            parts = [jnp.where(slot_here == k, x, zero) for k in range(slots)]
            slot_ids = lax.broadcasted_iota(jnp.int32, (slot_pad, CHUNK), 0)
            chosen = slot_ids == jnp.broadcast_to(slot, (slot_pad, CHUNK)).astype(jnp.int32)
            for axis in range(3):
                row = jnp.broadcast_to(fields[axis : axis + 1], (slot_pad, CHUNK))
                parts.append(jnp.where(chosen, row, 0.0).astype(jnp.bfloat16))
            place_ids = lax.broadcasted_iota(jnp.int32, (leaf_pts, CHUNK), 0)
            place = jnp.broadcast_to(fields[3:4].astype(jnp.int32), (leaf_pts, CHUNK))
            one_hot = jnp.where(place_ids == place, 1.0, 0.0).astype(jnp.bfloat16)
            total[...] += lax.dot_general(
                jnp.concatenate(parts, axis=0),
                one_hot,
                (((1,), (1,)), ((), ())),
                preferred_element_type=jnp.float32,
            )

    pairs = ((x_ref, x_all), (aux_ref, aux_all))
    for_each_block(lines, pairs, (send_sem, pass_sem, recv_sem), process)
    v_out[...] = total[: slots * rows, :].astype(jnp.bfloat16)
    c_out[...] = jnp.zeros_like(c_out)
    for slot in range(slots):
        for axis in range(3):
            at = slots * rows + axis * slot_pad + slot
            c_out[slot * 8 + axis : slot * 8 + axis + 1, :] = total[at : at + 1, :]


def arrange(lines, leaves, leaf_pts, x, aux):
    rows, dev_pts = x.shape
    devices = lines * 2
    slots = leaves + 2
    slot_pad = -(-slots // 8) * 8
    return pl.pallas_call(
        functools.partial(arrange_kernel, lines, leaves),
        out_shape=(
            jax.ShapeDtypeStruct((slots * rows, leaf_pts), jnp.bfloat16),
            jax.ShapeDtypeStruct((slots * 8, leaf_pts), jnp.float32),
        ),
        in_specs=[pl.BlockSpec(memory_space=pltpu.VMEM)] * 2,
        out_specs=(pl.BlockSpec(memory_space=pltpu.VMEM),) * 2,
        scratch_shapes=[
            pltpu.VMEM((devices,) + x.shape, jnp.bfloat16),
            pltpu.VMEM((devices,) + aux.shape, jnp.bfloat16),
            pltpu.VMEM((slots * rows + 3 * slot_pad, leaf_pts), jnp.float32),
            pltpu.SemaphoreType.DMA((2, lines)),
            pltpu.SemaphoreType.DMA((2, lines)),
            pltpu.SemaphoreType.DMA((2, devices)),
        ],
        compiler_params=pltpu.CompilerParams(
            collective_id=0, has_side_effects=True, vmem_limit_bytes=VMEM_LIMIT
        ),
        name="arrange",
    )(x, aux)


def hand_back_kernel(
    lines, leaves, y_ref, order_ref, out_ref, y_all, one_hot, leaf_at, send_sem, pass_sem, recv_sem
):
    leaf_pts = y_ref.shape[1]
    rows = y_ref.shape[0] // leaves
    dev_pts = order_ref.shape[1]
    order = order_ref[...]
    leaf_at[...] = order // leaf_pts
    for part in range(dev_pts // CHUNK):
        at = slice(part * CHUNK, (part + 1) * CHUNK)
        place_ids = lax.broadcasted_iota(jnp.int32, (leaf_pts, CHUNK), 0)
        place = jnp.broadcast_to(order[:, at] % leaf_pts, (leaf_pts, CHUNK))
        one_hot[:, at] = jnp.where(place_ids == place, 1.0, 0.0).astype(jnp.bfloat16)
    out_ref[...] = jnp.zeros_like(out_ref)

    def process(block):
        y = y_all[block]

        def chunk(part, carry):
            at = pl.ds(pl.multiple_of(part * CHUNK, CHUNK), CHUNK)
            found = jnp.dot(y, one_hot[:, at], preferred_element_type=jnp.float32)
            leaf = jnp.broadcast_to(leaf_at[:, at] - block * leaves, (rows, CHUNK))
            got = jnp.zeros((rows, CHUNK), jnp.float32)
            for k in range(leaves):
                got = jnp.where(leaf == k, found[k * rows : (k + 1) * rows], got)
            out_ref[:, at] += got.astype(jnp.bfloat16)
            return carry

        lax.fori_loop(0, dev_pts // CHUNK, chunk, 0)

    for_each_block(lines, ((y_ref, y_all),), (send_sem, pass_sem, recv_sem), process)


def hand_back(lines, leaves, y, order):
    devices = lines * 2
    rows = y.shape[0] // leaves
    dev_pts = order.shape[1]
    return pl.pallas_call(
        functools.partial(hand_back_kernel, lines, leaves),
        out_shape=jax.ShapeDtypeStruct((rows, dev_pts), jnp.bfloat16),
        in_specs=[pl.BlockSpec(memory_space=pltpu.VMEM)] * 2,
        out_specs=pl.BlockSpec(memory_space=pltpu.VMEM),
        scratch_shapes=[
            pltpu.VMEM((devices,) + y.shape, jnp.bfloat16),
            pltpu.VMEM((y.shape[1], dev_pts), jnp.bfloat16),
            pltpu.VMEM((1, dev_pts), jnp.int32),
            pltpu.SemaphoreType.DMA((1, lines)),
            pltpu.SemaphoreType.DMA((1, lines)),
            pltpu.SemaphoreType.DMA((1, devices)),
        ],
        compiler_params=pltpu.CompilerParams(
            collective_id=1, has_side_effects=True, vmem_limit_bytes=VMEM_LIMIT
        ),
        name="hand_back",
    )(y, order)


def matern(columns, rows):
    squared = None
    for axis in range(3):
        delta = columns[:, axis : axis + 1] - rows[axis : axis + 1, :]
        squared = delta * delta if squared is None else squared + delta * delta
    distance = squared * lax.rsqrt(jnp.maximum(squared, 1e-30))
    rate = ROOT_THREE / LENGTH_SCALE
    rising = KERNEL_GAIN + (KERNEL_GAIN * rate) * distance
    return (rising * jnp.exp2(distance * (-rate * LOG2_E))).astype(jnp.bfloat16)


def near_sums(leaves, v_ref, c_ref, near):
    rows = v_ref.shape[0] // (leaves + 2)
    near[...] = jnp.zeros_like(near)

    def vec_at(slot):
        return pl.ds(pl.multiple_of(slot * rows, rows), rows)

    def coord_at(slot):
        return pl.ds(pl.multiple_of(slot * 8, 8), 8)

    def step(slot, carry):
        here = c_ref[coord_at(slot), :]
        columns = jnp.transpose(here)
        beside = matern(columns, c_ref[coord_at(slot + 1), :])
        within = matern(columns, here)
        x_here = v_ref[vec_at(slot), :]
        x_next = v_ref[vec_at(slot + 1), :]
        near[vec_at(slot + 1), :] += jnp.dot(x_here, beside, preferred_element_type=jnp.float32)
        near[vec_at(slot), :] += jnp.dot(
            x_here, within, preferred_element_type=jnp.float32
        ) + lax.dot_general(
            x_next, beside, (((1,), (1,)), ((), ())), preferred_element_type=jnp.float32
        )
        return carry

    lax.fori_loop(0, leaves + 1, step, 0)


def near_kernel(
    lines,
    leaves,
    v_ref,
    c_ref,
    coef_ref,
    root_ref,
    near_out,
    levels_out,
    roots_out,
    near,
    send_sem,
    recv_sem,
    root_send,
    root_recv,
):
    devices = lines * 2
    nodes = coef_ref.shape[0]
    rows = v_ref.shape[0] // (leaves + 2)
    me = lax.axis_index("leaf") * 2 + lax.axis_index("sub")

    def place(device):
        return {"leaf": device // 2, "sub": lax.rem(device, 2)}

    after = lax.rem(me + 1, devices)
    before = lax.rem(me + devices - 1, devices)
    barrier = pltpu.get_barrier_semaphore()

    def greet(hop, carry):
        pl.semaphore_signal(
            barrier, inc=1, device_id=place(lax.rem(me + hop, devices)), device_id_type=MESH
        )
        return carry

    lax.fori_loop(1, devices, greet, 0)
    pl.semaphore_wait(barrier, devices - 1)

    def root_copy(hop):
        return pltpu.make_async_remote_copy(
            src_ref=root_ref,
            dst_ref=roots_out.at[me],
            send_sem=root_send.at[hop],
            recv_sem=root_recv.at[me],
            device_id=place(lax.rem(me + hop, devices)),
            device_id_type=MESH,
        )

    def start_root(hop, carry):
        root_copy(hop).start()
        return carry

    copies = [
        pltpu.make_async_remote_copy(
            src_ref=coef_ref,
            dst_ref=levels_out.at[which],
            send_sem=send_sem.at[which],
            recv_sem=recv_sem.at[which],
            device_id=place(target),
            device_id_type=MESH,
        )
        for which, target in ((0, after), (2, before))
    ]
    lax.fori_loop(1, devices, start_root, 0)
    for copy in copies:
        copy.start()
    levels_out[1] = coef_ref[...]
    roots_out[me] = root_ref[...]
    near_sums(leaves, v_ref, c_ref, near)
    near_out[...] = near[rows : (leaves + 1) * rows, :]

    def end_root(hop, carry):
        source = lax.rem(me + hop, devices)
        pltpu.make_async_remote_copy(
            src_ref=root_ref,
            dst_ref=roots_out.at[source],
            send_sem=root_send.at[hop],
            recv_sem=root_recv.at[source],
            device_id=place(source),
            device_id_type=MESH,
        ).wait()
        return carry

    lax.fori_loop(1, devices, end_root, 0)
    for copy in copies:
        copy.wait()


def near_and_levels(lines, leaves, v, c, coef, root):
    devices = lines * 2
    rows = v.shape[0] // (leaves + 2)
    return pl.pallas_call(
        functools.partial(near_kernel, lines, leaves),
        out_shape=(
            jax.ShapeDtypeStruct((leaves * rows, v.shape[1]), jnp.float32),
            jax.ShapeDtypeStruct((3,) + coef.shape, jnp.bfloat16),
            jax.ShapeDtypeStruct((devices,) + root.shape, jnp.bfloat16),
        ),
        in_specs=[pl.BlockSpec(memory_space=pltpu.VMEM)] * 4,
        out_specs=(pl.BlockSpec(memory_space=pltpu.VMEM),) * 3,
        scratch_shapes=[
            pltpu.VMEM(v.shape, jnp.float32),
            pltpu.SemaphoreType.DMA((3,)),
            pltpu.SemaphoreType.DMA((3,)),
            pltpu.SemaphoreType.DMA((devices,)),
            pltpu.SemaphoreType.DMA((devices,)),
        ],
        compiler_params=pltpu.CompilerParams(
            collective_id=2, has_side_effects=True, vmem_limit_bytes=VMEM_LIMIT
        ),
        name="near",
    )(v, c, coef, root)


def couple(couplings, gathered_rows):
    return jnp.einsum(
        "gkab,gkvb->gva", couplings, gathered_rows, preferred_element_type=jnp.float32
    )


def on_device(
    vectors,
    coords,
    point_order,
    leaf_basis,
    transfer_local,
    transfer_top,
    partners_local,
    coupling_local,
    top_partners,
    top_coupling,
):
    vec_rows = vectors.shape[0]
    dev_pts = vectors.shape[1]
    subtrees = lax.axis_size(("leaf", "sub"))
    leaves = leaf_basis.shape[0]
    rank_dim = leaf_basis.shape[1]
    leaf_pts = leaf_basis.shape[2]
    node_count = 2 * leaves - 1
    levels = leaves.bit_length()
    partners = partners_local.shape[1]
    top_count = top_partners.shape[1]
    my_index = lax.axis_index(("leaf", "sub"))
    lines = lax.axis_size("leaf")
    fields = jnp.concatenate(
        [
            coords,
            (point_order % leaf_pts)[None].astype(jnp.bfloat16),
            (point_order // leaf_pts % leaves)[None].astype(jnp.bfloat16),
            (point_order // dev_pts)[None].astype(jnp.bfloat16),
            jnp.zeros((FIELDS - 6, dev_pts), jnp.bfloat16),
        ],
        axis=0,
    )
    aux = fields.reshape(FIELDS, dev_pts // CHUNK, CHUNK).transpose(1, 0, 2)
    aux = aux.reshape(FIELDS * dev_pts // CHUNK, CHUNK)
    v_slots, c_slots = arrange(lines, leaves, leaf_pts, vectors, aux)
    leaf_rows = v_slots.reshape(leaves + 2, vec_rows, leaf_pts)[1 : leaves + 1]
    coefficients = jnp.einsum(
        "tvl,tal->tva", leaf_rows, leaf_basis, preferred_element_type=jnp.float32
    ).astype(jnp.bfloat16)
    transfers = transfer_local.reshape(2 * leaves - 2, rank_dim, rank_dim)
    couplings = coupling_local.reshape(node_count, partners, rank_dim, rank_dim)
    per_level = [coefficients]
    offset = 0
    level_count = leaves
    for level_idx in range(levels - 1):
        pair_mats = transfers[offset : offset + level_count].reshape(
            level_count // 2, 2, rank_dim, rank_dim
        )
        pair_coef = per_level[-1].reshape(level_count // 2, 2, vec_rows, rank_dim)
        per_level.append(
            jnp.einsum(
                "icab,icvb->iva", pair_mats, pair_coef, preferred_element_type=jnp.float32
            ).astype(jnp.bfloat16)
        )
        offset = offset + level_count
        level_count = level_count // 2
    all_levels = jnp.concatenate(per_level, axis=0)
    near_part, padded_all, stacked = near_and_levels(
        lines,
        leaves,
        v_slots,
        c_slots,
        all_levels.reshape(node_count * vec_rows, rank_dim),
        per_level[-1].reshape(vec_rows, rank_dim),
    )
    padded_all = padded_all.reshape(3 * node_count, vec_rows, rank_dim)
    local_idx = partners_local - (my_index - 1) * node_count
    local_out = couple(couplings, padded_all[local_idx])
    half_top = subtrees // 2
    quarter_top = subtrees // 4
    top_mats = transfer_top.reshape(subtrees + half_top, rank_dim, rank_dim)
    level_one = jnp.einsum(
        "icab,icvb->iva",
        top_mats[:subtrees].reshape(half_top, 2, rank_dim, rank_dim),
        stacked.reshape(half_top, 2, vec_rows, rank_dim),
        preferred_element_type=jnp.float32,
    ).astype(jnp.bfloat16)
    level_two = jnp.einsum(
        "icab,icvb->iva",
        top_mats[subtrees:].reshape(quarter_top, 2, rank_dim, rank_dim),
        level_one.reshape(quarter_top, 2, vec_rows, rank_dim),
        preferred_element_type=jnp.float32,
    ).astype(jnp.bfloat16)
    top_coef = jnp.concatenate([level_one, level_two], axis=0)
    level_shift = jnp.where(
        jnp.arange(half_top + quarter_top, dtype=jnp.int32)[:, None] >= half_top, half_top, 0
    ).astype(jnp.int32)
    top_out = couple(
        top_coupling.reshape(half_top + quarter_top, top_count, rank_dim, rank_dim),
        top_coef[top_partners + level_shift],
    )
    upper_bar = top_out[half_top:].astype(jnp.bfloat16)
    middle_top = top_out[:half_top] + jnp.einsum(
        "icab,iva->icvb",
        top_mats[subtrees:].reshape(quarter_top, 2, rank_dim, rank_dim),
        upper_bar,
        preferred_element_type=jnp.float32,
    ).reshape(half_top, vec_rows, rank_dim)
    middle_bar = middle_top.astype(jnp.bfloat16)
    mat_mine = lax.dynamic_index_in_dim(top_mats, my_index, 0, keepdims=False)
    parent_mine = lax.dynamic_index_in_dim(middle_bar, my_index // 2, 0, keepdims=False)
    root_down = jnp.einsum("ab,va->vb", mat_mine, parent_mine, preferred_element_type=jnp.float32)
    current = (local_out[node_count - 1] + root_down)[None]
    offset = node_count - 1
    level_count = 1
    for level_idx in range(levels - 1):
        child_count = level_count * 2
        offset = offset - child_count
        pair_mats = transfers[offset : offset + child_count].reshape(
            level_count, 2, rank_dim, rank_dim
        )
        downward = jnp.einsum(
            "icab,iva->icvb",
            pair_mats,
            current.astype(jnp.bfloat16),
            preferred_element_type=jnp.float32,
        ).reshape(child_count, vec_rows, rank_dim)
        current = local_out[offset : offset + child_count] + downward
        level_count = child_count
    far_field = jnp.einsum(
        "tva,tal->tvl", current.astype(jnp.bfloat16), leaf_basis, preferred_element_type=jnp.float32
    )
    answer = (far_field + near_part.reshape(far_field.shape)).astype(jnp.bfloat16)
    return hand_back(
        lines, leaves, answer.reshape(leaves * vec_rows, leaf_pts), point_order.reshape(1, dev_pts)
    )


def solution(mesh):
    in_specs = (
        P(("grp", "vec"), ("leaf", "sub")),
        P("grp", ("leaf", "sub")),
        P(("grp", "leaf", "sub")),
        P(("grp", "leaf", "sub"), None, None),
        P(("grp", "leaf", "sub"), None),
        P("grp", None),
        P(("grp", "leaf", "sub"), None),
        P(("grp", "leaf", "sub"), None, None),
        P("grp", None),
        P("grp", None, None),
    )
    out_specs = P(("grp", "vec"), ("leaf", "sub"))
    return jax.shard_map(
        on_device, mesh=mesh, in_specs=in_specs, out_specs=out_specs, check_vma=False
    )
```

profile of v0, /device:TPU:0, one launch (start us, length us, event | category | flops | bytes accessed | tf_op | source)
XLA Modules:
  0.0 118.2 jit_solution(7511273674557072982)
XLA Ops:
  0.0 0.8 fusion.25
  0.9 1.5 %concatenate.22 = bf16[8,4,1024]{2,0,1:T(8,128)(2,1)} concatenate(bf16[3,4,1024]{2,0,1:T(4,128)(2,1)} %bitcast.157, bf16[1,4,1024]{2,0,1:T(2,128)(2,1)S(1)} %concatenate.25, bf16[1,4,1024]{2,0,1:T(2,128)(2,1)S(1)} %concatenate.26, bf16[1,4,1024]{2,0,1:T(2,128)(2,1)S(1)} %concatenate.27, bf16[2,4,1024]{2,0,1:T(2,128)(2,1)S(1)} %broadcast_in_dim.20), dimensions={0} | concatenate | bytes 131072 | tf_op jit(solution)/shard_map/concatenate | solution.py:416
  2.4 41.7 %arrange.1 = (bf16[576,256]{1,0:T(8,128)(2,1)}, f32[144,256]{1,0:T(8,128)}) custom-call(bf16[32,4096]{1,0:T(8,128)(2,1)} %x_ref.1, bf16[32,1024]{1,0:T(8,128)(2,1)} %bitcast.151), custom_call_target="tpu_custom_call" | custom-call | tf_op jit(solution)/shard_map/arrange/pallas_call | solution.py:154
  44.1 1.0 slice.57
  45.1 0.3 constant_dynamic-update-slice_fusion.4
  45.4 0.2 reshape.131
  45.6 0.2 constant_dynamic-update-slice_fusion.3
  45.8 0.2 reshape.133
  46.0 0.2 constant_dynamic-update-slice_fusion.2
  46.3 0.1 constant_dynamic-update-slice_fusion.1
  46.6 0.7 constant_dynamic-update-slice_fusion
  47.4 0.7 copy-done.1
  48.1 21.3 %near.1 = (f32[512,256]{1,0:T(8,128)}, bf16[3,992,64]{2,1,0:T(8,128)(2,1)}, bf16[8,32,64]{2,1,0:T(8,128)(2,1)}) custom-call(bf16[576,256]{1,0:T(8,128)(2,1)} %get-tuple-element.10.v_ref, f32[144,256]{1,0:T(8,128)} %get-tuple-element.11.c_ref, bf16[992,64]{1,0:T(8,128)(2,1)} %bitcast.146, bf16[32,64]{1,0:T(8,128)(2,1)} %get-tuple-element.27.root_ref), custom_call_target="tpu_custom_call" | custom-call | tf_op jit(solution)/shard_map/near/pallas_call | solution.py:363
  69.8 0.6 pad_clamp_fusion
  70.4 2.8 %gather_fusion = bf16[124,32,64]{2,1,0:T(8,128)(2,1)} fusion(bf16[93,32,64]{2,1,0:T(8,128)(2,1)} %bitcast.143, s32[1024]{0:T(1024)S(1)} %get-tuple-element.29), kind=kCustom, calls=%fused_computation | custom fusion | bytes 1016304 | tf_op jit(solution)/shard_map/gather | solution.py:461
  73.3 3.2 %reshape.139 = bf16[31,4,64,64]{3,2,1,0:T(8,128)(2,1)S(1)} reshape(bf16[31,4,4096]{2,1,0:T(4,128)(2,1)} %param.17) | data formatting | bytes 2031616 | tf_op jit(solution)/shard_map/reshape | solution.py:434
  76.5 1.9 %convolution_bitcast_fusion = f32[31,32,64]{2,1,0:T(8,128)S(1)} fusion(bf16[31,4,32,64]{3,2,1,0:T(8,128)(2,1)} %bitcast.142, bf16[31,4,64,64]{3,2,1,0:T(8,128)(2,1)S(1)} %reshape.139), kind=kOutput, calls=%fused_computation.3 | convolution fusion | flops 32505856 | bytes 1777664 | tf_op jit(solution)/shard_map/gkab,gkvb->gva/dot_general | solution.py:387
  78.4 1.1 reshape.146
  79.7 0.8 slice.68
  80.5 0.2 reshape.141
  80.7 1.0 fusion.3
  81.7 0.1 fusion.6
  81.9 0.7 gather_fusion.1
  82.6 1.1 reshape.144
  83.7 0.2 convolution_bitcast_fusion.2
  83.9 0.1 fusion.27
  84.2 0.2 fusion.12
  84.4 0.1 fusion.19
  84.6 0.2 fusion.16
  84.8 0.9 fusion
  85.7 30.7 %hand_back.1 = bf16[32,4096]{1,0:T(8,128)(2,1)} custom-call(bf16[512,256]{1,0:T(8,128)(2,1)} %bitcast.145, s32[1,4096]{1,0:T(1,128)} %bitcast.156), custom_call_target="tpu_custom_call" | custom-call | tf_op jit(solution)/shard_map/hand_back/pallas_call | solution.py:214
  116.5 1.7 %copy.36 = bf16[32,4096]{1,0:T(8,128)(2,1)} copy(bf16[32,4096]{1,0:T(8,128)(2,1)} %hand_back.1) | data formatting | bytes 524288
  (44 shorter events, 1.1 us)
Async XLA Ops:
  0.0 45.1 %copy-start = (bf16[16,64,256]{2,1,0:T(8,128)(2,1)S(1)}, bf16[16,64,256]{2,1,0:T(8,128)(2,1)}, u32[]{:S(2)}) copy-start(bf16[16,64,256]{2,1,0:T(8,128)(2,1)} %param.13) | copy-start | bytes 1572868
  0.0 45.4 %slice-start = ((bf16[30,4096]{1,0:T(8,128)(2,1)}), bf16[16,4096]{1,0:T(8,128)(2,1)S(1)}, s32[]{:S(2)}) async-start(bf16[30,4096]{1,0:T(8,128)(2,1)} %param.14), calls=%async_computation | async-start | bytes 262144 | tf_op jit(solution)/shard_map/slice | solution.py:439
  0.0 45.8 %slice-start.1 = ((bf16[30,4096]{1,0:T(8,128)(2,1)}), bf16[8,4096]{1,0:T(8,128)(2,1)S(1)}, s32[]{:S(2)}) async-start(bf16[30,4096]{1,0:T(8,128)(2,1)} %param.14), calls=%async_computation.1 | async-start | bytes 131072 | tf_op jit(solution)/shard_map/slice | solution.py:439
  0.0 46.2 %slice-start.2 = ((bf16[30,4096]{1,0:T(8,128)(2,1)}), bf16[4,4096]{1,0:T(4,128)(2,1)S(1)}, s32[]{:S(2)}) async-start(bf16[30,4096]{1,0:T(8,128)(2,1)} %param.14), calls=%async_computation.2 | async-start | bytes 65536 | tf_op jit(solution)/shard_map/slice | solution.py:439
  2.4 44.1 %copy-start.2 = (bf16[30,4096]{1,0:T(8,128)(2,1)S(1)}, bf16[30,4096]{1,0:T(8,128)(2,1)}, u32[]{:S(2)}) copy-start(bf16[30,4096]{1,0:T(8,128)(2,1)} %param.14) | copy-start | bytes 737284
  45.1 24.4 %copy-start.7 = (s32[6,2]{0,1:T(2,128)S(1)}, s32[6,2]{0,1:T(2,128)}, u32[]{:S(2)}) copy-start(s32[6,2]{0,1:T(2,128)} %param.18) | copy-start | bytes 148
  45.1 24.5 %copy-start.6 = (s32[31,4]{0,1:T(4,128)S(1)}, s32[31,4]{0,1:T(4,128)}, u32[]{:S(2)}) copy-start(s32[31,4]{0,1:T(4,128)} %param.16) | copy-start | bytes 1492
  46.6 26.6 %copy-start.4 = (bf16[2,64,64]{2,1,0:T(8,128)(2,1)}, bf16[2,64,64]{2,1,0:T(8,128)(2,1)S(1)}, u32[]{:S(2)}) copy-start(bf16[2,64,64]{2,1,0:T(8,128)(2,1)S(1)} %reshape.136) | copy-start | bytes 49156
  47.4 0.7 copy-start.1
  76.5 3.0 %slice-start.3 = ((bf16[12,4096]{1,0:T(8,128)(2,1)}), bf16[4,4096]{1,0:T(4,128)(2,1)S(1)}, s32[]{:S(2)}) async-start(bf16[12,4096]{1,0:T(8,128)(2,1)} %param.15), calls=%async_computation.3 | async-start | bytes 65536 | tf_op jit(solution)/shard_map/slice | solution.py:473
  78.4 5.8 %copy-start.5 = (bf16[2,64,64]{2,1,0:T(8,128)(2,1)S(1)}, bf16[2,64,64]{2,1,0:T(8,128)(2,1)}, u32[]{:S(2)}) copy-start(bf16[2,64,64]{2,1,0:T(8,128)(2,1)} %copy-done.4) | copy-start | bytes 49156
  80.7 4.1 %copy-start.3 = (f32[512,256]{1,0:T(8,128)S(1)}, f32[512,256]{1,0:T(8,128)}, u32[]{:S(2)}) copy-start(f32[512,256]{1,0:T(8,128)} %get-tuple-element.14) | copy-start | bytes 1572868
where the time goes:
time: 120 us; the launch traced here: 118 us
  Pallas kernels  93.8 us (78%)
  local copies, waits for them, and re-layouts  16.1 us (13%)
  matrix products  6.47 us (5%)
  other arithmetic  1.56 us (1%)
    pallas_call x1, Pallas kernels, arrange(): pl.pallas_call(functools.partial(arrange_kernel, lines, leaves), out_shap...  41.7 us
    pallas_call x1, Pallas kernels, hand_back(): pl.pallas_call(functools.partial(hand_back_kernel, lines, leaves), out_sh...  30.7 us
    pallas_call x1, Pallas kernels, near_and_levels(): pl.pallas_call(functools.partial(near_kernel, lines, leaves), out_shape=(...  21.3 us
    reshape x1, local copies, waits for them, and re-layouts, on_device(): couplings = coupling_local.reshape(node_count, partners, rank_dim, rank_dim)  3.22 us
    gather x1, local copies, waits for them, and re-layouts, on_device(): local_out = couple(couplings, padded_all[local_idx])  2.82 us

commit v1 on v0

--- a/solution.py
+++ b/solution.py
@@ -14,7 +14,8 @@
 MESH = pl.DeviceIdType.MESH
 VMEM_LIMIT = 56 * 1024 * 1024
 CHUNK = 1024
-FIELDS = 8
+FIELDS = 6
+AUX_CHUNK = 512
 
 
 def for_each_block(lines, pairs, sems, process):
@@ -22,83 +23,102 @@
     mine = lax.axis_index("leaf")
     core = lax.axis_index("sub")
     other = 1 - core
-    me = mine * 2 + core
     barrier = pltpu.get_barrier_semaphore()
-    for hop in range(1, lines):
-        target = lax.rem(mine + hop, lines)
-        pl.semaphore_signal(barrier, inc=1, device_id={"leaf": target}, device_id_type=MESH)
-    pl.semaphore_signal(barrier, inc=1, device_id={"sub": other}, device_id_type=MESH)
-    pl.semaphore_wait(barrier, lines)
-
-    def sends(hop):
-        target = lax.rem(mine + hop, lines)
+
+    def greet(target):
+        pl.semaphore_signal(barrier, inc=1, device_id=target, device_id_type=MESH)
+
+    def copies(block, target, sem):
         return [
             pltpu.make_async_remote_copy(
-                src_ref=own,
-                dst_ref=held.at[me],
-                send_sem=send_sem.at[which, hop],
-                recv_sem=recv_sem.at[which, me],
-                device_id={"leaf": target},
+                src_ref=held.at[block],
+                dst_ref=held.at[block],
+                send_sem=sem.at[which, block],
+                recv_sem=recv_sem.at[which, block],
+                device_id=target,
                 device_id_type=MESH,
             )
             for which, (own, held) in enumerate(pairs)
         ]
 
-    def across(hop, block):
-        return [
-            pltpu.make_async_remote_copy(
-                src_ref=held.at[block],
-                dst_ref=held.at[block],
-                send_sem=pass_sem.at[which, hop],
-                recv_sem=recv_sem.at[which, block],
-                device_id={"sub": other},
-                device_id_type=MESH,
+    def ahead(block, way):
+        return copies(block, {"leaf": mine + way}, send_sem.at[(way + 1) // 2])
+
+    def across(block):
+        return copies(block, {"sub": other}, pass_sem)
+
+    def has(way):
+        return mine > 0 if way < 0 else mine < lines - 1
+
+    def guarded(condition, action):
+        pl.when(condition)(action)
+
+    def start(some):
+        for copy in some:
+            copy.start()
+
+    def wait_sent(some):
+        for copy in some:
+            copy.wait_send()
+
+    def wait_here(some):
+        for copy in some:
+            copy.wait_recv()
+
+    greet({"sub": other})
+    for way in (-1, 1):
+        guarded(has(way), lambda way=way: greet({"leaf": mine + way}))
+    for own, held in pairs:
+        held[mine * 2 + core] = own[...]
+    inside = jnp.logical_and(has(-1), has(1))
+    guarded(inside, lambda: pl.semaphore_wait(barrier, 3))
+    guarded(jnp.logical_not(inside), lambda: pl.semaphore_wait(barrier, 2))
+
+    me = mine * 2 + core
+    for way in (-1, 1):
+        guarded(has(way), lambda way=way: start(ahead(me, way)))
+    start(across(me))
+    process(me)
+    wait_here(across(mine * 2 + other))
+    process(mine * 2 + other)
+
+    def step(hop, carry):
+        for way in (-1, 1):
+            line = mine - way * hop
+            there = line >= 0 if way > 0 else line < lines
+            block = line * 2 + core
+
+            def take(way=way, block=block):
+                wait_here(across(block))
+                guarded(has(way), lambda: start(ahead(block, way)))
+                start(across(block))
+
+            guarded(there, take)
+        for way in (-1, 1):
+            line = mine - way * hop
+            there = line >= 0 if way > 0 else line < lines
+
+            def use(line=line):
+                process(line * 2 + core)
+                wait_here(across(line * 2 + other))
+                process(line * 2 + other)
+
+            guarded(there, use)
+        return carry
+
+    lax.fori_loop(1, lines, step, 0)
+
+    def finish(line, carry):
+        block = line * 2 + core
+        wait_sent(across(block))
+        for way in (-1, 1):
+            upstream = line <= mine if way > 0 else line >= mine
+            guarded(
+                jnp.logical_and(upstream, has(way)), lambda way=way: wait_sent(ahead(block, way))
             )
-            for which, (own, held) in enumerate(pairs)
-        ]
-
-    def begin(hop, carry):
-        for copy in sends(hop):
-            copy.start()
         return carry
 
-    lax.fori_loop(1, lines, begin, 0)
-    for own, held in pairs:
-        held[me] = own[...]
-
-    def step(hop, carry):
-        line = lax.rem(mine + lines - hop, lines)
-        near_block = line * 2 + core
-        far_block = line * 2 + other
-
-        @pl.when(hop > 0)
-        def _():
-            for copy in across(hop, near_block):
-                copy.wait_recv()
-
-        for copy in across(hop, near_block):
-            copy.start()
-        process(near_block)
-        for copy in across(hop, far_block):
-            copy.wait_recv()
-        process(far_block)
-        return carry
-
-    lax.fori_loop(0, lines, step, 0)
-
-    def finish(hop, carry):
-        for copy in sends(hop):
-            copy.wait_send()
-        return carry
-
-    lax.fori_loop(1, lines, finish, 0)
-
-    def finish_across(hop, carry):
-        for copy in across(hop, lax.rem(mine + lines - hop, lines) * 2 + core):
-            copy.wait_send()
-        return carry
-
-    lax.fori_loop(0, lines, finish_across, 0)
+    lax.fori_loop(0, lines, finish, 0)
 
 
 def arrange_kernel(
@@ -109,48 +129,55 @@
     dev_pts = x_ref.shape[1]
     leaf_pts = v_out.shape[1]
     slots = leaves + 2
-    slot_pad = -(-slots // 8) * 8
+    slot_pad = -(-slots // 16) * 16
     total[...] = jnp.zeros_like(total)
+    slot_ids = lax.broadcasted_iota(jnp.int32, (slot_pad, CHUNK), 0).astype(jnp.bfloat16)
+    place_ids = lax.broadcasted_iota(jnp.int32, (leaf_pts, CHUNK), 0).astype(jnp.bfloat16)
 
     def process(block):
         aux = aux_all[block].astype(jnp.float32)
         for part in range(dev_pts // CHUNK):
-            fields = aux[part * FIELDS : (part + 1) * FIELDS]
+            at = part * FIELDS * CHUNK // AUX_CHUNK
+            fields = jnp.concatenate(
+                [aux[at + k : at + k + FIELDS] for k in range(0, FIELDS * CHUNK // AUX_CHUNK, FIELDS)],
+                axis=1,
+            )
             x = x_all[block, :, part * CHUNK : (part + 1) * CHUNK]
             slot = (fields[5:6] - me.astype(jnp.float32)) * leaves + fields[4:5] + 1.0
-            slot_here = jnp.broadcast_to(slot, (rows, CHUNK)).astype(jnp.int32)
+            slot = jnp.clip(slot, -1.0, float(slots)).astype(jnp.bfloat16)
+            slot_here = jnp.broadcast_to(slot, (rows, CHUNK))
             zero = jnp.zeros_like(x)
-            parts = [jnp.where(slot_here == k, x, zero) for k in range(slots)]
-            slot_ids = lax.broadcasted_iota(jnp.int32, (slot_pad, CHUNK), 0)
-            chosen = slot_ids == jnp.broadcast_to(slot, (slot_pad, CHUNK)).astype(jnp.int32)
+            parts = [jnp.where(slot_here == jnp.bfloat16(k), x, zero) for k in range(slots)]
+            chosen = slot_ids == jnp.broadcast_to(slot, (slot_pad, CHUNK))
             for axis in range(3):
-                row = jnp.broadcast_to(fields[axis : axis + 1], (slot_pad, CHUNK))
-                parts.append(jnp.where(chosen, row, 0.0).astype(jnp.bfloat16))
-            place_ids = lax.broadcasted_iota(jnp.int32, (leaf_pts, CHUNK), 0)
-            place = jnp.broadcast_to(fields[3:4].astype(jnp.int32), (leaf_pts, CHUNK))
-            one_hot = jnp.where(place_ids == place, 1.0, 0.0).astype(jnp.bfloat16)
+                row = fields[axis : axis + 1].astype(jnp.bfloat16)
+                row = jnp.broadcast_to(row, (slot_pad, CHUNK))
+                parts.append(jnp.where(chosen, row, jnp.zeros_like(row)))
+            place = jnp.broadcast_to(fields[3:4].astype(jnp.bfloat16), (leaf_pts, CHUNK))
+            one_hot = jnp.where(place_ids == place, jnp.bfloat16(1), jnp.bfloat16(0))
             total[...] += lax.dot_general(
                 jnp.concatenate(parts, axis=0),
                 one_hot,
                 (((1,), (1,)), ((), ())),
                 preferred_element_type=jnp.float32,
-            )
+            ).astype(jnp.bfloat16)
 
     pairs = ((x_ref, x_all), (aux_ref, aux_all))
     for_each_block(lines, pairs, (send_sem, pass_sem, recv_sem), process)
-    v_out[...] = total[: slots * rows, :].astype(jnp.bfloat16)
+    v_out[...] = total[: slots * rows, :]
+    found = total[slots * rows :, :].astype(jnp.float32)
     c_out[...] = jnp.zeros_like(c_out)
     for slot in range(slots):
         for axis in range(3):
-            at = slots * rows + axis * slot_pad + slot
-            c_out[slot * 8 + axis : slot * 8 + axis + 1, :] = total[at : at + 1, :]
+            at = axis * slot_pad + slot
+            c_out[slot * 8 + axis : slot * 8 + axis + 1, :] = found[at : at + 1, :]
 
 
 def arrange(lines, leaves, leaf_pts, x, aux):
     rows, dev_pts = x.shape
     devices = lines * 2
     slots = leaves + 2
-    slot_pad = -(-slots // 8) * 8
+    slot_pad = -(-slots // 16) * 16
     return pl.pallas_call(
         functools.partial(arrange_kernel, lines, leaves),
         out_shape=(
@@ -162,9 +189,9 @@
         scratch_shapes=[
             pltpu.VMEM((devices,) + x.shape, jnp.bfloat16),
             pltpu.VMEM((devices,) + aux.shape, jnp.bfloat16),
-            pltpu.VMEM((slots * rows + 3 * slot_pad, leaf_pts), jnp.float32),
-            pltpu.SemaphoreType.DMA((2, lines)),
-            pltpu.SemaphoreType.DMA((2, lines)),
+            pltpu.VMEM((slots * rows + 3 * slot_pad, leaf_pts), jnp.bfloat16),
+            pltpu.SemaphoreType.DMA((2, 2, devices)),
+            pltpu.SemaphoreType.DMA((2, devices)),
             pltpu.SemaphoreType.DMA((2, devices)),
         ],
         compiler_params=pltpu.CompilerParams(
@@ -181,7 +208,7 @@
     rows = y_ref.shape[0] // leaves
     dev_pts = order_ref.shape[1]
     order = order_ref[...]
-    leaf_at[...] = order // leaf_pts
+    leaf_at[...] = (order // leaf_pts).astype(jnp.float32)
     for part in range(dev_pts // CHUNK):
         at = slice(part * CHUNK, (part + 1) * CHUNK)
         place_ids = lax.broadcasted_iota(jnp.int32, (leaf_pts, CHUNK), 0)
@@ -195,11 +222,14 @@
         def chunk(part, carry):
             at = pl.ds(pl.multiple_of(part * CHUNK, CHUNK), CHUNK)
             found = jnp.dot(y, one_hot[:, at], preferred_element_type=jnp.float32)
-            leaf = jnp.broadcast_to(leaf_at[:, at] - block * leaves, (rows, CHUNK))
-            got = jnp.zeros((rows, CHUNK), jnp.float32)
+            leaf = leaf_at[:, at] - (block * leaves).astype(jnp.float32)
+            leaf = jnp.clip(leaf, -1.0, float(leaves)).astype(jnp.bfloat16)
+            leaf = jnp.broadcast_to(leaf, (rows, CHUNK))
+            got = jnp.zeros((rows, CHUNK), jnp.bfloat16)
             for k in range(leaves):
-                got = jnp.where(leaf == k, found[k * rows : (k + 1) * rows], got)
-            out_ref[:, at] += got.astype(jnp.bfloat16)
+                here = found[k * rows : (k + 1) * rows].astype(jnp.bfloat16)
+                got = jnp.where(leaf == jnp.bfloat16(k), here, got)
+            out_ref[:, at] += got
             return carry
 
         lax.fori_loop(0, dev_pts // CHUNK, chunk, 0)
@@ -219,9 +249,9 @@
         scratch_shapes=[
             pltpu.VMEM((devices,) + y.shape, jnp.bfloat16),
             pltpu.VMEM((y.shape[1], dev_pts), jnp.bfloat16),
-            pltpu.VMEM((1, dev_pts), jnp.int32),
-            pltpu.SemaphoreType.DMA((1, lines)),
-            pltpu.SemaphoreType.DMA((1, lines)),
+            pltpu.VMEM((1, dev_pts), jnp.float32),
+            pltpu.SemaphoreType.DMA((2, 1, devices)),
+            pltpu.SemaphoreType.DMA((1, devices)),
             pltpu.SemaphoreType.DMA((1, devices)),
         ],
         compiler_params=pltpu.CompilerParams(
@@ -419,12 +449,11 @@
             (point_order % leaf_pts)[None].astype(jnp.bfloat16),
             (point_order // leaf_pts % leaves)[None].astype(jnp.bfloat16),
             (point_order // dev_pts)[None].astype(jnp.bfloat16),
-            jnp.zeros((FIELDS - 6, dev_pts), jnp.bfloat16),
         ],
         axis=0,
     )
-    aux = fields.reshape(FIELDS, dev_pts // CHUNK, CHUNK).transpose(1, 0, 2)
-    aux = aux.reshape(FIELDS * dev_pts // CHUNK, CHUNK)
+    aux = fields.reshape(FIELDS, dev_pts // AUX_CHUNK, AUX_CHUNK).transpose(1, 0, 2)
+    aux = aux.reshape(FIELDS * dev_pts // AUX_CHUNK, AUX_CHUNK)
     v_slots, c_slots = arrange(lines, leaves, leaf_pts, vectors, aux)
     leaf_rows = v_slots.reshape(leaves + 2, vec_rows, leaf_pts)[1 : leaves + 1]
     coefficients = jnp.einsum(

time: 120 us -> 101 us (0.84); the launches traced: 118 us -> 101 us
  Pallas kernels: 93.8 us -> 76.5 us
    pallas_call x1, Pallas kernels: 41.7 us -> 33.3 us  [arrange(): pl.pallas_call(functools.partial(arrange_kernel, lines, leaves), out_shap...]
    pallas_call x1, Pallas kernels: 21.3 us -> 14 us  [near_and_levels(): pl.pallas_call(functools.partial(near_kernel, lines, leaves), out_shape=(...]
    pallas_call x1, Pallas kernels: 30.7 us -> 29.2 us  [hand_back(): pl.pallas_call(functools.partial(hand_back_kernel, lines, leaves), out_sh...]
    concatenate x4 -> x3, local copies, waits for them, and re-layouts: 1.53 us -> 0.03 us  [on_device(): jnp.concatenate([coords, (point_order % leaf_pts)[None].astype(jnp.bfloat...]
where the time goes in v1:
time: 101 us
  Pallas kernels  76.5 us (76%)
  local copies, waits for them, and re-layouts  15.2 us (15%)
  matrix products  6.46 us (6%)
  other arithmetic  2.4 us (2%)
    pallas_call x1, Pallas kernels, arrange(): pl.pallas_call(functools.partial(arrange_kernel, lines, leaves), out_shap...  33.3 us
    pallas_call x1, Pallas kernels, hand_back(): pl.pallas_call(functools.partial(hand_back_kernel, lines, leaves), out_sh...  29.2 us
    pallas_call x1, Pallas kernels, near_and_levels(): pl.pallas_call(functools.partial(near_kernel, lines, leaves), out_shape=(...  14 us
    reshape x1, local copies, waits for them, and re-layouts, on_device(): couplings = coupling_local.reshape(node_count, partners, rank_dim, rank_dim)  3.22 us
    gather x1, local copies, waits for them, and re-layouts, on_device(): local_out = couple(couplings, padded_all[local_idx])  2.82 us
    unnamed x17, local copies, waits for them, and re-layouts  2.4 us
    dot_general x2, matrix products, couple(): jnp.einsum('gkab,gkvb->gva', couplings, gathered_rows, preferred_element_...  2.03 us

profile of v1, /device:TPU:0, one launch (start us, length us, event | category | flops | bytes accessed | tf_op | source)
XLA Modules:
  0.0 100.9 jit_solution(13482204532857160705)
XLA Ops:
  0.0 0.8 fusion.21
  0.9 0.8 maximum_bitcast_fusion
  1.7 0.6 reshape.128.aux_ref
  2.4 33.3 %arrange.1 = (bf16[576,256]{1,0:T(8,128)(2,1)}, f32[144,256]{1,0:T(8,128)}) custom-call(bf16[32,4096]{1,0:T(8,128)(2,1)} %x_ref.1, bf16[48,512]{1,0:T(8,128)(2,1)} %reshape.128.aux_ref), custom_call_target="tpu_custom_call" | custom-call | tf_op jit(solution)/shard_map/arrange/pallas_call | solution.py:181
  35.7 1.0 slice.57
  36.7 0.3 constant_dynamic-update-slice_fusion.4
  37.0 0.2 reshape.130
  37.3 0.2 constant_dynamic-update-slice_fusion.3
  37.5 0.2 reshape.132
  37.7 0.2 constant_dynamic-update-slice_fusion.2
  38.0 0.1 constant_dynamic-update-slice_fusion.1
  38.3 0.7 constant_dynamic-update-slice_fusion
  39.0 0.7 copy-done.1
  39.7 14.0 %near.1 = (f32[512,256]{1,0:T(8,128)}, bf16[3,992,64]{2,1,0:T(8,128)(2,1)}, bf16[8,32,64]{2,1,0:T(8,128)(2,1)}) custom-call(bf16[576,256]{1,0:T(8,128)(2,1)} %get-tuple-element.10.v_ref, f32[144,256]{1,0:T(8,128)} %get-tuple-element.11.c_ref, bf16[992,64]{1,0:T(8,128)(2,1)} %bitcast.145, bf16[32,64]{1,0:T(8,128)(2,1)} %get-tuple-element.27.root_ref), custom_call_target="tpu_custom_call" | custom-call | tf_op jit(solution)/shard_map/near/pallas_call | solution.py:393
  54.1 0.6 pad_clamp_fusion
  54.7 2.8 %gather_fusion = bf16[124,32,64]{2,1,0:T(8,128)(2,1)} fusion(bf16[93,32,64]{2,1,0:T(8,128)(2,1)} %bitcast.142, s32[1024]{0:T(1024)S(1)} %get-tuple-element.29), kind=kCustom, calls=%fused_computation | custom fusion | bytes 1016304 | tf_op jit(solution)/shard_map/gather | solution.py:490
  57.6 3.2 %reshape.138 = bf16[31,4,64,64]{3,2,1,0:T(8,128)(2,1)S(1)} reshape(bf16[31,4,4096]{2,1,0:T(4,128)(2,1)} %param.17) | data formatting | bytes 2031616 | tf_op jit(solution)/shard_map/reshape | solution.py:463
  60.8 1.9 %convolution_bitcast_fusion = f32[31,32,64]{2,1,0:T(8,128)S(1)} fusion(bf16[31,4,32,64]{3,2,1,0:T(8,128)(2,1)} %bitcast.141, bf16[31,4,64,64]{3,2,1,0:T(8,128)(2,1)S(1)} %reshape.138), kind=kOutput, calls=%fused_computation.3 | convolution fusion | flops 32505856 | bytes 1777664 | tf_op jit(solution)/shard_map/gkab,gkvb->gva/dot_general | solution.py:417
  62.7 1.1 %reshape.145 = bf16[12,64,64]{2,1,0:T(8,128)(2,1)S(1)} reshape(bf16[12,4096]{1,0:T(8,128)(2,1)} %param.15) | data formatting | bytes 196608 | tf_op jit(solution)/shard_map/reshape | solution.py:493
  64.0 0.8 slice.68
  64.8 0.2 reshape.140
  65.0 1.0 %fusion.3 = bf16[4,32,64]{2,1,0:T(8,128)(2,1)S(1)} fusion(bf16[4,2,32,64]{3,2,1,0:T(8,128)(2,1)} %bitcast.153, bf16[4,2,64,64]{3,2,1,0:T(8,128)(2,1)S(1)} %reshape.140), kind=kOutput, calls=%fused_computation.12 | convolution fusion | flops 2105344 | bytes 114688 | tf_op jit(solution)/shard_map/icab,icvb->iva/dot_general | solution.py:494
  66.0 0.1 fusion.6
  66.2 0.7 gather_fusion.1
  66.9 1.1 %reshape.143 = bf16[6,2,64,64]{3,2,1,0:T(8,128)(2,1)S(1)} reshape(bf16[6,2,4096]{2,1,0:T(2,128)(2,1)} %param.19) | data formatting | bytes 196608 | tf_op jit(solution)/shard_map/reshape | solution.py:511
  68.0 0.2 convolution_bitcast_fusion.2
  68.2 0.1 fusion.27
  68.5 0.2 fusion.12
  68.9 0.2 fusion.16
  69.1 0.9 fusion
  70.0 29.2 %hand_back.1 = bf16[32,4096]{1,0:T(8,128)(2,1)} custom-call(bf16[512,256]{1,0:T(8,128)(2,1)} %bitcast.144, s32[1,4096]{1,0:T(1,128)} %bitcast.154), custom_call_target="tpu_custom_call" | custom-call | tf_op jit(solution)/shard_map/hand_back/pallas_call | solution.py:244
  99.2 1.7 %copy.36 = bf16[32,4096]{1,0:T(8,128)(2,1)} copy(bf16[32,4096]{1,0:T(8,128)(2,1)} %hand_back.1) | data formatting | bytes 524288
  (44 shorter events, 1.2 us)
Async XLA Ops:
  0.0 36.7 %copy-start = (bf16[16,64,256]{2,1,0:T(8,128)(2,1)S(1)}, bf16[16,64,256]{2,1,0:T(8,128)(2,1)}, u32[]{:S(2)}) copy-start(bf16[16,64,256]{2,1,0:T(8,128)(2,1)} %param.13) | copy-start | bytes 1572868
  0.0 37.0 %slice-start = ((bf16[30,4096]{1,0:T(8,128)(2,1)}), bf16[16,4096]{1,0:T(8,128)(2,1)S(1)}, s32[]{:S(2)}) async-start(bf16[30,4096]{1,0:T(8,128)(2,1)} %param.14), calls=%async_computation | async-start | bytes 262144 | tf_op jit(solution)/shard_map/slice | solution.py:468
  0.0 37.5 %slice-start.1 = ((bf16[30,4096]{1,0:T(8,128)(2,1)}), bf16[8,4096]{1,0:T(8,128)(2,1)S(1)}, s32[]{:S(2)}) async-start(bf16[30,4096]{1,0:T(8,128)(2,1)} %param.14), calls=%async_computation.1 | async-start | bytes 131072 | tf_op jit(solution)/shard_map/slice | solution.py:468
  0.8 37.0 %slice-start.2 = ((bf16[30,4096]{1,0:T(8,128)(2,1)}), bf16[4,4096]{1,0:T(4,128)(2,1)S(1)}, s32[]{:S(2)}) async-start(bf16[30,4096]{1,0:T(8,128)(2,1)} %param.14), calls=%async_computation.2 | async-start | bytes 65536 | tf_op jit(solution)/shard_map/slice | solution.py:468
  1.7 36.4 %copy-start.2 = (bf16[30,4096]{1,0:T(8,128)(2,1)S(1)}, bf16[30,4096]{1,0:T(8,128)(2,1)}, u32[]{:S(2)}) copy-start(bf16[30,4096]{1,0:T(8,128)(2,1)} %param.14) | copy-start | bytes 737284
  36.7 17.0 %copy-start.7 = (s32[6,2]{0,1:T(2,128)S(1)}, s32[6,2]{0,1:T(2,128)}, u32[]{:S(2)}) copy-start(s32[6,2]{0,1:T(2,128)} %param.18) | copy-start | bytes 148
  36.7 17.2 %copy-start.6 = (s32[31,4]{0,1:T(4,128)S(1)}, s32[31,4]{0,1:T(4,128)}, u32[]{:S(2)}) copy-start(s32[31,4]{0,1:T(4,128)} %param.16) | copy-start | bytes 1492
  38.3 19.3 %copy-start.4 = (bf16[2,64,64]{2,1,0:T(8,128)(2,1)}, bf16[2,64,64]{2,1,0:T(8,128)(2,1)S(1)}, u32[]{:S(2)}) copy-start(bf16[2,64,64]{2,1,0:T(8,128)(2,1)S(1)} %reshape.135) | copy-start | bytes 49156
  39.0 0.7 copy-start.1
  60.8 3.0 %slice-start.3 = ((bf16[12,4096]{1,0:T(8,128)(2,1)}), bf16[4,4096]{1,0:T(4,128)(2,1)S(1)}, s32[]{:S(2)}) async-start(bf16[12,4096]{1,0:T(8,128)(2,1)} %param.15), calls=%async_computation.3 | async-start | bytes 65536 | tf_op jit(solution)/shard_map/slice | solution.py:502
  62.7 5.8 %copy-start.5 = (bf16[2,64,64]{2,1,0:T(8,128)(2,1)S(1)}, bf16[2,64,64]{2,1,0:T(8,128)(2,1)}, u32[]{:S(2)}) copy-start(bf16[2,64,64]{2,1,0:T(8,128)(2,1)} %copy-done.4) | copy-start | bytes 49156
  65.0 4.1 %copy-start.3 = (f32[512,256]{1,0:T(8,128)S(1)}, f32[512,256]{1,0:T(8,128)}, u32[]{:S(2)}) copy-start(f32[512,256]{1,0:T(8,128)} %get-tuple-element.14) | copy-start | bytes 1572868

commit v2 on v1

--- a/solution.py
+++ b/solution.py
@@ -18,7 +18,15 @@
 AUX_CHUNK = 512
 
 
-def for_each_block(lines, pairs, sems, process):
+def cut_rows(rows):
+    return rows // 2 if rows % 32 == 0 else rows
+
+
+def piece_count(arrays):
+    return sum(a.shape[0] // cut_rows(a.shape[0]) for a in arrays)
+
+
+def for_each_block(lines, pairs, sems, process, prepare):
     send_sem, pass_sem, recv_sem = sems
     mine = lax.axis_index("leaf")
     core = lax.axis_index("sub")
@@ -28,17 +36,22 @@
     def greet(target):
         pl.semaphore_signal(barrier, inc=1, device_id=target, device_id_type=MESH)
 
+    pieces = []
+    for own, held in pairs:
+        cut = cut_rows(own.shape[0])
+        pieces += [(held, pl.ds(at, cut)) for at in range(0, own.shape[0], cut)]
+
     def copies(block, target, sem):
         return [
             pltpu.make_async_remote_copy(
-                src_ref=held.at[block],
-                dst_ref=held.at[block],
+                src_ref=held.at[block, rows],
+                dst_ref=held.at[block, rows],
                 send_sem=sem.at[which, block],
                 recv_sem=recv_sem.at[which, block],
                 device_id=target,
                 device_id_type=MESH,
             )
-            for which, (own, held) in enumerate(pairs)
+            for which, (held, rows) in enumerate(pieces)
         ]
 
     def ahead(block, way):
@@ -78,6 +91,7 @@
     for way in (-1, 1):
         guarded(has(way), lambda way=way: start(ahead(me, way)))
     start(across(me))
+    prepare()
     process(me)
     wait_here(across(mine * 2 + other))
     process(mine * 2 + other)
@@ -89,9 +103,10 @@
             block = line * 2 + core
 
             def take(way=way, block=block):
-                wait_here(across(block))
-                guarded(has(way), lambda: start(ahead(block, way)))
-                start(across(block))
+                for which, passed in enumerate(across(block)):
+                    passed.wait_recv()
+                    guarded(has(way), lambda which=which: ahead(block, way)[which].start())
+                    passed.start()
 
             guarded(there, take)
         for way in (-1, 1):
@@ -130,7 +145,10 @@
     leaf_pts = v_out.shape[1]
     slots = leaves + 2
     slot_pad = -(-slots // 16) * 16
-    total[...] = jnp.zeros_like(total)
+
+    def prepare():
+        total[...] = jnp.zeros_like(total)
+
     slot_ids = lax.broadcasted_iota(jnp.int32, (slot_pad, CHUNK), 0).astype(jnp.bfloat16)
     place_ids = lax.broadcasted_iota(jnp.int32, (leaf_pts, CHUNK), 0).astype(jnp.bfloat16)
 
@@ -163,7 +181,7 @@
             ).astype(jnp.bfloat16)
 
     pairs = ((x_ref, x_all), (aux_ref, aux_all))
-    for_each_block(lines, pairs, (send_sem, pass_sem, recv_sem), process)
+    for_each_block(lines, pairs, (send_sem, pass_sem, recv_sem), process, prepare)
     v_out[...] = total[: slots * rows, :]
     found = total[slots * rows :, :].astype(jnp.float32)
     c_out[...] = jnp.zeros_like(c_out)
@@ -190,9 +208,9 @@
             pltpu.VMEM((devices,) + x.shape, jnp.bfloat16),
             pltpu.VMEM((devices,) + aux.shape, jnp.bfloat16),
             pltpu.VMEM((slots * rows + 3 * slot_pad, leaf_pts), jnp.bfloat16),
-            pltpu.SemaphoreType.DMA((2, 2, devices)),
-            pltpu.SemaphoreType.DMA((2, devices)),
-            pltpu.SemaphoreType.DMA((2, devices)),
+            pltpu.SemaphoreType.DMA((2, piece_count([x, aux]), devices)),
+            pltpu.SemaphoreType.DMA((piece_count([x, aux]), devices)),
+            pltpu.SemaphoreType.DMA((piece_count([x, aux]), devices)),
         ],
         compiler_params=pltpu.CompilerParams(
             collective_id=0, has_side_effects=True, vmem_limit_bytes=VMEM_LIMIT
@@ -207,14 +225,17 @@
     leaf_pts = y_ref.shape[1]
     rows = y_ref.shape[0] // leaves
     dev_pts = order_ref.shape[1]
-    order = order_ref[...]
-    leaf_at[...] = (order // leaf_pts).astype(jnp.float32)
-    for part in range(dev_pts // CHUNK):
-        at = slice(part * CHUNK, (part + 1) * CHUNK)
-        place_ids = lax.broadcasted_iota(jnp.int32, (leaf_pts, CHUNK), 0)
-        place = jnp.broadcast_to(order[:, at] % leaf_pts, (leaf_pts, CHUNK))
-        one_hot[:, at] = jnp.where(place_ids == place, 1.0, 0.0).astype(jnp.bfloat16)
-    out_ref[...] = jnp.zeros_like(out_ref)
+
+    def prepare():
+        place_ids = lax.broadcasted_iota(jnp.int32, (leaf_pts, CHUNK), 0).astype(jnp.bfloat16)
+        for part in range(dev_pts // CHUNK):
+            at = slice(part * CHUNK, (part + 1) * CHUNK)
+            order = order_ref[:, at]
+            leaf_at[:, at] = (order // leaf_pts).astype(jnp.float32)
+            place = (order % leaf_pts).astype(jnp.float32).astype(jnp.bfloat16)
+            place = jnp.broadcast_to(place, (leaf_pts, CHUNK))
+            one_hot[:, at] = jnp.where(place_ids == place, jnp.bfloat16(1), jnp.bfloat16(0))
+        out_ref[...] = jnp.zeros_like(out_ref)
 
     def process(block):
         y = y_all[block]
@@ -234,7 +255,8 @@
 
         lax.fori_loop(0, dev_pts // CHUNK, chunk, 0)
 
-    for_each_block(lines, ((y_ref, y_all),), (send_sem, pass_sem, recv_sem), process)
+    sems = (send_sem, pass_sem, recv_sem)
+    for_each_block(lines, ((y_ref, y_all),), sems, process, prepare)
 
 
 def hand_back(lines, leaves, y, order):
@@ -250,9 +272,9 @@
             pltpu.VMEM((devices,) + y.shape, jnp.bfloat16),
             pltpu.VMEM((y.shape[1], dev_pts), jnp.bfloat16),
             pltpu.VMEM((1, dev_pts), jnp.float32),
-            pltpu.SemaphoreType.DMA((2, 1, devices)),
-            pltpu.SemaphoreType.DMA((1, devices)),
-            pltpu.SemaphoreType.DMA((1, devices)),
+            pltpu.SemaphoreType.DMA((2, piece_count([y]), devices)),
+            pltpu.SemaphoreType.DMA((piece_count([y]), devices)),
+            pltpu.SemaphoreType.DMA((piece_count([y]), devices)),
         ],
         compiler_params=pltpu.CompilerParams(
             collective_id=1, has_side_effects=True, vmem_limit_bytes=VMEM_LIMIT
@@ -308,7 +330,7 @@
     coef_ref,
     root_ref,
     near_out,
-    levels_out,
+    levels,
     roots_out,
     near,
     send_sem,
@@ -354,7 +376,7 @@
     copies = [
         pltpu.make_async_remote_copy(
             src_ref=coef_ref,
-            dst_ref=levels_out.at[which],
+            dst_ref=levels.at[which],
             send_sem=send_sem.at[which],
             recv_sem=recv_sem.at[which],
             device_id=place(target),
@@ -365,7 +387,7 @@
     lax.fori_loop(1, devices, start_root, 0)
     for copy in copies:
         copy.start()
-    levels_out[1] = coef_ref[...]
+    levels[1] = coef_ref[...]
     roots_out[me] = root_ref[...]
     near_sums(leaves, v_ref, c_ref, near)
     near_out[...] = near[rows : (leaves + 1) * rows, :]
@@ -385,6 +407,70 @@
     lax.fori_loop(1, devices, end_root, 0)
     for copy in copies:
         copy.wait()
+
+
+def couple_kernel(rows, levels, weight_ref, partner_ref, coupled_out, weights):
+    pairs_total = weight_ref.shape[0]
+    rank_dim = levels.shape[1]
+    pair_rows = rank_dim // 2
+    for k in range(pair_rows):
+        part = weight_ref[:, k * 2 * rank_dim : (k + 1) * 2 * rank_dim]
+        weights[k * pairs_total : (k + 1) * pairs_total, :] = part.astype(jnp.float32)
+
+    node_total = coupled_out.shape[0] // rows
+    partners = pairs_total // node_total
+    mixed = lax.broadcasted_iota(jnp.int32, (rank_dim, rank_dim), 0)
+    wanted = lax.broadcasted_iota(jnp.int32, (rank_dim, rank_dim), 1)
+    even = jnp.logical_and(mixed < pair_rows, wanted == 2 * mixed)
+    odd = jnp.logical_and(mixed >= pair_rows, wanted == 2 * (mixed - pair_rows) + 1)
+    unmix = jnp.where(jnp.logical_or(even, odd), 1.0, 0.0).astype(jnp.bfloat16)
+
+    def node(index, carry):
+        low = jnp.zeros((rows, pair_rows), jnp.float32)
+        high = jnp.zeros((rows, pair_rows), jnp.float32)
+        for k in range(partners):
+            pair = index * partners + k
+            matrix = weights[pl.ds(pair, pair_rows, stride=pairs_total), :].astype(jnp.bfloat16)
+            number = partner_ref[pair]
+            x = levels[pl.ds(pl.multiple_of(number * rows, rows), rows), :]
+            dims = (((1,), (1,)), ((), ()))
+            low += lax.dot_general(
+                x, matrix[:, :rank_dim], dims, preferred_element_type=jnp.float32
+            )
+            high += lax.dot_general(
+                x, matrix[:, rank_dim:], dims, preferred_element_type=jnp.float32
+            )
+        both = jnp.concatenate([low, high], axis=1)
+        coupled_out[pl.ds(pl.multiple_of(index * rows, rows), rows), :] = both
+        return carry
+
+    lax.fori_loop(0, node_total, node, 0)
+    both = coupled_out[...]
+    upper = both.astype(jnp.bfloat16)
+    lower = (both - upper.astype(jnp.float32)).astype(jnp.bfloat16)
+    coupled_out[...] = jnp.dot(upper, unmix, preferred_element_type=jnp.float32) + jnp.dot(
+        lower, unmix, preferred_element_type=jnp.float32
+    )
+
+
+def couple_local(rows, levels, weights, partners):
+    pairs_total, entries = weights.shape
+    rank_dim = levels.shape[1]
+    return pl.pallas_call(
+        functools.partial(couple_kernel, rows),
+        out_shape=jax.ShapeDtypeStruct((levels.shape[0] // 3, rank_dim), jnp.float32),
+        in_specs=[
+            pl.BlockSpec(memory_space=pltpu.VMEM),
+            pl.BlockSpec(memory_space=pltpu.VMEM),
+            pl.BlockSpec(memory_space=pltpu.SMEM),
+        ],
+        out_specs=pl.BlockSpec(memory_space=pltpu.VMEM),
+        scratch_shapes=[
+            pltpu.VMEM((pairs_total * entries // (2 * rank_dim), 2 * rank_dim), jnp.float32)
+        ],
+        compiler_params=pltpu.CompilerParams(vmem_limit_bytes=VMEM_LIMIT),
+        name="couple",
+    )(levels, weights, partners)
 
 
 def near_and_levels(lines, leaves, v, c, coef, root):
@@ -460,7 +546,6 @@
         "tvl,tal->tva", leaf_rows, leaf_basis, preferred_element_type=jnp.float32
     ).astype(jnp.bfloat16)
     transfers = transfer_local.reshape(2 * leaves - 2, rank_dim, rank_dim)
-    couplings = coupling_local.reshape(node_count, partners, rank_dim, rank_dim)
     per_level = [coefficients]
     offset = 0
     level_count = leaves
@@ -477,6 +562,7 @@
         offset = offset + level_count
         level_count = level_count // 2
     all_levels = jnp.concatenate(per_level, axis=0)
+    local_idx = partners_local - (my_index - 1) * node_count
     near_part, padded_all, stacked = near_and_levels(
         lines,
         leaves,
@@ -485,9 +571,14 @@
         all_levels.reshape(node_count * vec_rows, rank_dim),
         per_level[-1].reshape(vec_rows, rank_dim),
     )
-    padded_all = padded_all.reshape(3 * node_count, vec_rows, rank_dim)
-    local_idx = partners_local - (my_index - 1) * node_count
-    local_out = couple(couplings, padded_all[local_idx])
+    local_out = couple_local(
+        vec_rows,
+        padded_all.reshape(3 * node_count * vec_rows, rank_dim),
+        coupling_local.reshape(node_count * partners, rank_dim * rank_dim),
+        local_idx.reshape(node_count * partners),
+    )
+    local_out = local_out.reshape(node_count, vec_rows, rank_dim)
+    stacked = stacked.reshape(subtrees, vec_rows, rank_dim)
     half_top = subtrees // 2
     quarter_top = subtrees // 4
     top_mats = transfer_top.reshape(subtrees + half_top, rank_dim, rank_dim)

time: 101 us -> 114 us (1.13)
  Pallas kernels: 76.5 us -> 89.3 us
  local copies, waits for them, and re-layouts: 15.2 us -> 19 us
  matrix products: 6.46 us -> 3.69 us
  other arithmetic: 2.4 us -> 1.01 us
    pallas_call x0 -> x1, Pallas kernels: none -> 11.6 us  [couple_local(): pl.pallas_call(functools.partial(couple_kernel, rows), out_shape=jax.Shap...]
    unnamed x17 -> x25, local copies, waits for them, and re-layouts: 2.4 us -> 6.98 us
    gather x1 -> x0, local copies, waits for them, and re-layouts: 2.82 us -> none  [on_device(): local_out = couple(couplings, padded_all[local_idx])]
    slice x0 -> x8, local copies, waits for them, and re-layouts: none -> 2.74 us  [on_device(): current = local_out[offset:offset + child_count] + downward]
    slice x7, local copies, waits for them, and re-layouts: 0.04 us -> 2.11 us  [on_device(): transfers[offset:offset + level_count]]
    dot_general x2 -> x1, matrix products: 2.03 us -> 0.16 us  [couple(): jnp.einsum('gkab,gkvb->gva', couplings, gathered_rows, preferred_element_...]
    reshape x1 -> x2, local copies, waits for them, and re-layouts: 3.22 us -> 1.82 us  [the longest x1 1.21 us: on_device(): coupling_local.reshape(node_count * partners, rank_dim * rank_dim)]
    pallas_call x1, Pallas kernels: 29.2 us -> 30.4 us  [hand_back(): pl.pallas_call(functools.partial(hand_back_kernel, lines, leaves), out_sh...]
where the time goes in v2:
time: 114 us; the launch traced here: 113 us
  Pallas kernels  89.3 us (78%)
  local copies, waits for them, and re-layouts  19 us (17%)
  matrix products  3.69 us (3%)
    pallas_call x1, Pallas kernels, arrange(): pl.pallas_call(functools.partial(arrange_kernel, lines, leaves), out_shap...  34 us
    pallas_call x1, Pallas kernels, hand_back(): pl.pallas_call(functools.partial(hand_back_kernel, lines, leaves), out_sh...  30.4 us
    pallas_call x1, Pallas kernels, near_and_levels(): pl.pallas_call(functools.partial(near_kernel, lines, leaves), out_shape=(...  13.3 us
    pallas_call x1, Pallas kernels, couple_local(): pl.pallas_call(functools.partial(couple_kernel, rows), out_shape=jax.Shap...  11.6 us
    unnamed x25, local copies, waits for them, and re-layouts  6.98 us
    slice x8, local copies, waits for them, and re-layouts, on_device(): current = local_out[offset:offset + child_count] + downward  2.74 us

profile of v2, /device:TPU:0, one launch (start us, length us, event | category | flops | bytes accessed | tf_op | source)
XLA Modules:
  0.0 113.4 jit_solution(7977994994902093381)
XLA Ops:
  0.0 0.8 fusion.20
  0.9 0.7 copy-done.9
  1.7 0.6 reshape.138.aux_ref
  2.3 34.0 %arrange.1 = (bf16[576,256]{1,0:T(8,128)(2,1)}, f32[144,256]{1,0:T(8,128)}) custom-call(bf16[32,4096]{1,0:T(8,128)(2,1)} %x_ref.1, bf16[48,512]{1,0:T(8,128)(2,1)} %reshape.138.aux_ref), custom_call_target="tpu_custom_call" | custom-call | tf_op jit(solution)/shard_map/arrange/pallas_call | solution.py:199
  36.3 1.0 slice.70
  37.3 0.3 constant_dynamic-update-slice_fusion.4
  37.6 0.9 slice-done.4
  39.0 0.4 slice-done.5
  39.7 0.8 slice-done.6
  40.9 0.7 constant_dynamic-update-slice_fusion
  41.7 0.7 copy-done.3
  42.4 13.3 %near.1 = (f32[512,256]{1,0:T(8,128)}, bf16[3,992,64]{2,1,0:T(8,128)(2,1)}, bf16[8,32,64]{2,1,0:T(8,128)(2,1)}) custom-call(bf16[576,256]{1,0:T(8,128)(2,1)} %get-tuple-element.10.v_ref, f32[144,256]{1,0:T(8,128)} %get-tuple-element.11.c_ref, bf16[992,64]{1,0:T(8,128)(2,1)} %bitcast.148, bf16[32,64]{1,0:T(8,128)(2,1)} %get-tuple-element.27.root_ref), custom_call_target="tpu_custom_call" | custom-call | tf_op jit(solution)/shard_map/near/pallas_call | solution.py:479
  55.7 1.2 %reshape.148.weight_ref = bf16[124,4096]{1,0:T(8,128)(2,1)} reshape(bf16[31,4,4096]{2,1,0:T(4,128)(2,1)S(1)} %copy-done.2) | data formatting | bytes 2031616 | tf_op jit(solution)/shard_map/reshape | solution.py:577
  56.9 0.7 copy-done.10
  57.6 0.6 reshape.149.partner_ref
  58.3 11.6 %couple.1 = f32[992,64]{1,0:T(8,128)} custom-call(bf16[2976,64]{1,0:T(8,128)(2,1)} %bitcast.147, bf16[124,4096]{1,0:T(8,128)(2,1)} %reshape.148.weight_ref, s32[124]{0:T(128)} %reshape.149.partner_ref), custom_call_target="tpu_custom_call" | custom-call | tf_op jit(solution)/shard_map/couple/pallas_call | solution.py:459
  69.9 0.9 copy-done.6
  71.0 0.8 slice-done.7
  71.9 0.8 slice-done.8
  72.9 0.7 copy-done.8
  73.9 0.7 copy-done.11
  74.8 0.6 gather_fusion
  75.3 0.3 copy-done.7
  76.2 0.5 copy-done.1
  76.8 0.6 slice-done.3
  77.5 0.2 fusion.12
  77.7 0.6 slice-done.2
  78.5 0.8 slice-done.1
  79.4 0.8 slice-done
  80.4 0.9 fusion
  81.3 30.4 %hand_back.1 = bf16[32,4096]{1,0:T(8,128)(2,1)} custom-call(bf16[512,256]{1,0:T(8,128)(2,1)} %bitcast.146, s32[1,4096]{1,0:T(1,128)} %bitcast.157), custom_call_target="tpu_custom_call" | custom-call | tf_op jit(solution)/shard_map/hand_back/pallas_call | solution.py:266
  111.7 1.7 %copy.35 = bf16[32,4096]{1,0:T(8,128)(2,1)} copy(bf16[32,4096]{1,0:T(8,128)(2,1)} %hand_back.1) | data formatting | bytes 524288
  (60 shorter events, 3.6 us)
Async XLA Ops:
  0.0 37.3 %copy-start = (bf16[16,64,256]{2,1,0:T(8,128)(2,1)S(1)}, bf16[16,64,256]{2,1,0:T(8,128)(2,1)}, u32[]{:S(2)}) copy-start(bf16[16,64,256]{2,1,0:T(8,128)(2,1)} %param.13) | copy-start | bytes 1572868
  0.8 0.8 copy-start.9
  37.6 0.9 slice-start.4
  38.5 0.8 slice-start.5
  38.7 16.9 %copy-start.2 = (bf16[31,4,4096]{2,1,0:T(4,128)(2,1)S(1)}, bf16[31,4,4096]{2,1,0:T(4,128)(2,1)}, u32[]{:S(2)}) copy-start(bf16[31,4,4096]{2,1,0:T(4,128)(2,1)} %param.17) | copy-start | bytes 3047428
  39.7 0.8 slice-start.6
  39.7 1.1 copy-start.4
  41.7 0.7 copy-start.3
  56.9 0.7 copy-start.10
  69.9 0.9 copy-start.6
  71.0 0.8 slice-start.7
  71.9 0.8 slice-start.8
  72.7 0.8 copy-start.8
  73.9 0.7 copy-start.11
  74.8 0.9 copy-start.7
  75.7 1.0 copy-start.1
  76.7 0.8 slice-start.3
  77.5 0.8 slice-start.2
  78.3 0.9 slice-start.1
  79.2 1.0 slice-start
  79.2 1.1 copy-start.5

commit v3 on v1

--- a/solution.py
+++ b/solution.py
@@ -12,13 +12,13 @@
 KERNEL_GAIN = 0.25
 LOG2_E = 1.4426950408889634
 MESH = pl.DeviceIdType.MESH
-VMEM_LIMIT = 56 * 1024 * 1024
+VMEM_LIMIT = 24 * 1024 * 1024
 CHUNK = 1024
 FIELDS = 6
 AUX_CHUNK = 512
 
 
-def for_each_block(lines, pairs, sems, process):
+def for_each_block(lines, pairs, sems, process, prepare):
     send_sem, pass_sem, recv_sem = sems
     mine = lax.axis_index("leaf")
     core = lax.axis_index("sub")
@@ -78,6 +78,7 @@
     for way in (-1, 1):
         guarded(has(way), lambda way=way: start(ahead(me, way)))
     start(across(me))
+    prepare()
     process(me)
     wait_here(across(mine * 2 + other))
     process(mine * 2 + other)
@@ -130,7 +131,10 @@
     leaf_pts = v_out.shape[1]
     slots = leaves + 2
     slot_pad = -(-slots // 16) * 16
-    total[...] = jnp.zeros_like(total)
+
+    def prepare():
+        total[...] = jnp.zeros_like(total)
+
     slot_ids = lax.broadcasted_iota(jnp.int32, (slot_pad, CHUNK), 0).astype(jnp.bfloat16)
     place_ids = lax.broadcasted_iota(jnp.int32, (leaf_pts, CHUNK), 0).astype(jnp.bfloat16)
 
@@ -163,7 +167,7 @@
             ).astype(jnp.bfloat16)
 
     pairs = ((x_ref, x_all), (aux_ref, aux_all))
-    for_each_block(lines, pairs, (send_sem, pass_sem, recv_sem), process)
+    for_each_block(lines, pairs, (send_sem, pass_sem, recv_sem), process, prepare)
     v_out[...] = total[: slots * rows, :]
     found = total[slots * rows :, :].astype(jnp.float32)
     c_out[...] = jnp.zeros_like(c_out)
@@ -207,14 +211,17 @@
     leaf_pts = y_ref.shape[1]
     rows = y_ref.shape[0] // leaves
     dev_pts = order_ref.shape[1]
-    order = order_ref[...]
-    leaf_at[...] = (order // leaf_pts).astype(jnp.float32)
-    for part in range(dev_pts // CHUNK):
-        at = slice(part * CHUNK, (part + 1) * CHUNK)
-        place_ids = lax.broadcasted_iota(jnp.int32, (leaf_pts, CHUNK), 0)
-        place = jnp.broadcast_to(order[:, at] % leaf_pts, (leaf_pts, CHUNK))
-        one_hot[:, at] = jnp.where(place_ids == place, 1.0, 0.0).astype(jnp.bfloat16)
-    out_ref[...] = jnp.zeros_like(out_ref)
+
+    def prepare():
+        place_ids = lax.broadcasted_iota(jnp.int32, (leaf_pts, CHUNK), 0).astype(jnp.bfloat16)
+        for part in range(dev_pts // CHUNK):
+            at = slice(part * CHUNK, (part + 1) * CHUNK)
+            order = order_ref[:, at]
+            leaf_at[:, at] = (order // leaf_pts).astype(jnp.float32)
+            place = (order % leaf_pts).astype(jnp.float32).astype(jnp.bfloat16)
+            place = jnp.broadcast_to(place, (leaf_pts, CHUNK))
+            one_hot[:, at] = jnp.where(place_ids == place, jnp.bfloat16(1), jnp.bfloat16(0))
+        out_ref[...] = jnp.zeros_like(out_ref)
 
     def process(block):
         y = y_all[block]
@@ -234,7 +241,8 @@
 
         lax.fori_loop(0, dev_pts // CHUNK, chunk, 0)
 
-    for_each_block(lines, ((y_ref, y_all),), (send_sem, pass_sem, recv_sem), process)
+    sems = (send_sem, pass_sem, recv_sem)
+    for_each_block(lines, ((y_ref, y_all),), sems, process, prepare)
 
 
 def hand_back(lines, leaves, y, order):

time: 101 us -> 91.5 us (0.906)
  Pallas kernels: 76.5 us -> 70.8 us
  local copies, waits for them, and re-layouts: 15.2 us -> 13 us
  matrix products: 6.46 us -> 5.05 us
    pallas_call x1, Pallas kernels: 14 us -> 11.8 us  [near_and_levels(): pl.pallas_call(functools.partial(near_kernel, lines, leaves), out_shape=(...]
    pallas_call x1, Pallas kernels: 29.2 us -> 27.4 us  [hand_back(): pl.pallas_call(functools.partial(hand_back_kernel, lines, leaves), out_sh...]
    pallas_call x1, Pallas kernels: 33.3 us -> 31.6 us  [arrange(): pl.pallas_call(functools.partial(arrange_kernel, lines, leaves), out_shap...]
    gather x1, local copies, waits for them, and re-layouts: 2.82 us -> 1.69 us  [on_device(): local_out = couple(couplings, padded_all[local_idx])]
    unnamed x17 -> x23, local copies, waits for them, and re-layouts: 2.4 us -> 2.17 us
where the time goes in v3:
time: 91.5 us; the launch traced here: 91.1 us
  Pallas kernels  70.8 us (77%)
  local copies, waits for them, and re-layouts  13 us (14%)
  matrix products  5.05 us (6%)
  other arithmetic  1.79 us (2%)
    pallas_call x1, Pallas kernels, arrange(): pl.pallas_call(functools.partial(arrange_kernel, lines, leaves), out_shap...  31.6 us
    pallas_call x1, Pallas kernels, hand_back(): pl.pallas_call(functools.partial(hand_back_kernel, lines, leaves), out_sh...  27.4 us
    pallas_call x1, Pallas kernels, near_and_levels(): pl.pallas_call(functools.partial(near_kernel, lines, leaves), out_shape=(...  11.8 us
    reshape x1, local copies, waits for them, and re-layouts, on_device(): couplings = coupling_local.reshape(node_count, partners, rank_dim, rank_dim)  3.21 us
    dot_general x2, matrix products, couple(): jnp.einsum('gkab,gkvb->gva', couplings, gathered_rows, preferred_element_...  2.81 us
    unnamed x23, local copies, waits for them, and re-layouts  2.17 us

profile of v3, /device:TPU:0, one launch (start us, length us, event | category | flops | bytes accessed | tf_op | source)
XLA Modules:
  0.0 91.1 jit_solution(18032851916366654535)
XLA Ops:
  0.0 0.8 fusion.21
  0.9 0.8 maximum_bitcast_fusion
  1.8 0.9 %copy-done.1 = bf16[32,4096]{1,0:T(8,128)(2,1)S(1)} copy-done((bf16[32,4096]{1,0:T(8,128)(2,1)S(1)}, bf16[32,4096]{1,0:T(8,128)(2,1)}, u32[]{:S(2)}) %copy-start.1) | copy-done | bytes 262168
  2.7 31.6 %arrange.1 = (bf16[576,256]{1,0:T(8,128)(2,1)S(1)}, f32[144,256]{1,0:T(8,128)S(1)}) custom-call(bf16[32,4096]{1,0:T(8,128)(2,1)S(1)} %copy-done.1, bf16[48,512]{1,0:T(8,128)(2,1)S(1)} %reshape.128.aux_ref), custom_call_target="tpu_custom_call" | custom-call | tf_op jit(solution)/shard_map/arrange/pallas_call | solution.py:185
  34.4 0.3 constant_dynamic-update-slice_fusion.4
  34.7 0.2 reshape.130
  35.0 0.2 constant_dynamic-update-slice_fusion.3
  35.2 0.2 reshape.132
  35.4 0.2 constant_dynamic-update-slice_fusion.2
  35.7 0.1 constant_dynamic-update-slice_fusion.1
  36.1 0.2 copy-done.4
  36.3 0.3 copy-done.7
  36.6 11.8 %near.1 = (f32[512,256]{1,0:T(8,128)S(1)}, bf16[3,992,64]{2,1,0:T(8,128)(2,1)S(1)}, bf16[8,32,64]{2,1,0:T(8,128)(2,1)S(1)}) custom-call(bf16[576,256]{1,0:T(8,128)(2,1)S(1)} %get-tuple-element.10.v_ref, f32[144,256]{1,0:T(8,128)S(1)} %get-tuple-element.11.c_ref, bf16[992,64]{1,0:T(8,128)(2,1)S(1)} %bitcast.143, bf16[32,64]{1,0:T(8,128)(2,1)S(1)} %get-tuple-element.27.root_ref), custom_call_target="tpu_custom_call" | custom-call | tf_op jit(solution)/shard_map/near/pallas_call | solution.py:401
  48.9 1.7 %gather_fusion = bf16[124,32,64]{2,1,0:T(8,128)(2,1)} fusion(bf16[93,32,64]{2,1,0:T(8,128)(2,1)S(1)} %bitcast.141, s32[1024]{0:T(1024)S(1)} %get-tuple-element.29), kind=kCustom, calls=%fused_computation | custom fusion | bytes 1016304 | tf_op jit(solution)/shard_map/gather | solution.py:498
  50.5 3.2 %reshape.138 = bf16[31,4,64,64]{3,2,1,0:T(8,128)(2,1)S(1)} reshape(bf16[31,4,4096]{2,1,0:T(4,128)(2,1)} %param.17) | data formatting | bytes 2031616 | tf_op jit(solution)/shard_map/reshape | solution.py:471
  53.8 2.7 %convolution_bitcast_fusion = f32[31,32,64]{2,1,0:T(8,128)} fusion(bf16[31,4,32,64]{3,2,1,0:T(8,128)(2,1)} %bitcast.147, bf16[31,4,64,64]{3,2,1,0:T(8,128)(2,1)S(1)} %reshape.138), kind=kOutput, calls=%fused_computation.3 | convolution fusion | flops 32505856 | bytes 1777664 | tf_op jit(solution)/shard_map/gkab,gkvb->gva/dot_general | solution.py:425
  56.4 1.2 %reshape.145 = bf16[12,64,64]{2,1,0:T(8,128)(2,1)S(1)} reshape(bf16[12,4096]{1,0:T(8,128)(2,1)} %param.15) | data formatting | bytes 196608 | tf_op jit(solution)/shard_map/reshape | solution.py:501
  57.6 0.9 slice.69
  58.6 0.8 slice.68
  59.5 0.2 reshape.140
  59.6 0.1 fusion.3
  59.8 0.1 fusion.6
  60.0 0.6 gather_fusion.1
  60.5 1.1 %reshape.143 = bf16[6,2,64,64]{3,2,1,0:T(8,128)(2,1)S(1)} reshape(bf16[6,2,4096]{2,1,0:T(2,128)(2,1)} %param.19) | data formatting | bytes 196608 | tf_op jit(solution)/shard_map/reshape | solution.py:519
  61.6 0.2 convolution_bitcast_fusion.2
  61.8 0.1 fusion.27
  62.1 0.2 fusion.12
  62.4 0.1 fusion.19
  62.5 0.2 fusion.16
  62.8 0.2 fusion
  63.0 27.4 %hand_back.1 = bf16[32,4096]{1,0:T(8,128)(2,1)S(1)} custom-call(bf16[512,256]{1,0:T(8,128)(2,1)S(1)} %bitcast.142, s32[1,4096]{1,0:T(1,128)S(1)} %bitcast.146), custom_call_target="tpu_custom_call" | custom-call | tf_op jit(solution)/shard_map/hand_back/pallas_call | solution.py:252
  90.4 0.7 copy.36
  (49 shorter events, 1.3 us)
Async XLA Ops:
  0.0 34.4 %copy-start = (bf16[16,64,256]{2,1,0:T(8,128)(2,1)S(1)}, bf16[16,64,256]{2,1,0:T(8,128)(2,1)}, u32[]{:S(2)}) copy-start(bf16[16,64,256]{2,1,0:T(8,128)(2,1)} %param.13) | copy-start | bytes 1572868
  0.0 34.7 %slice-start = ((bf16[30,4096]{1,0:T(8,128)(2,1)}), bf16[16,4096]{1,0:T(8,128)(2,1)S(1)}, s32[]{:S(2)}) async-start(bf16[30,4096]{1,0:T(8,128)(2,1)} %param.14), calls=%async_computation | async-start | bytes 262144 | tf_op jit(solution)/shard_map/slice | solution.py:476
  0.0 35.2 %slice-start.1 = ((bf16[30,4096]{1,0:T(8,128)(2,1)}), bf16[8,4096]{1,0:T(8,128)(2,1)S(1)}, s32[]{:S(2)}) async-start(bf16[30,4096]{1,0:T(8,128)(2,1)} %param.14), calls=%async_computation.1 | async-start | bytes 131072 | tf_op jit(solution)/shard_map/slice | solution.py:476
  0.8 34.7 %slice-start.2 = ((bf16[30,4096]{1,0:T(8,128)(2,1)}), bf16[4,4096]{1,0:T(4,128)(2,1)S(1)}, s32[]{:S(2)}) async-start(bf16[30,4096]{1,0:T(8,128)(2,1)} %param.14), calls=%async_computation.2 | async-start | bytes 65536 | tf_op jit(solution)/shard_map/slice | solution.py:476
  1.8 1.0 %copy-start.1 = (bf16[32,4096]{1,0:T(8,128)(2,1)S(1)}, bf16[32,4096]{1,0:T(8,128)(2,1)}, u32[]{:S(2)}) copy-start(bf16[32,4096]{1,0:T(8,128)(2,1)} %x_ref.1) | copy-start | bytes 786436
  2.7 33.1 %copy-start.6 = (bf16[30,4096]{1,0:T(8,128)(2,1)S(1)}, bf16[30,4096]{1,0:T(8,128)(2,1)}, u32[]{:S(2)}) copy-start(bf16[30,4096]{1,0:T(8,128)(2,1)} %param.14) | copy-start | bytes 737284
  34.4 14.0 %copy-start.10 = (s32[6,2]{0,1:T(2,128)S(1)}, s32[6,2]{0,1:T(2,128)}, u32[]{:S(2)}) copy-start(s32[6,2]{0,1:T(2,128)} %param.18) | copy-start | bytes 148
  34.4 14.2 %copy-start.9 = (s32[31,4]{0,1:T(4,128)S(1)}, s32[31,4]{0,1:T(4,128)}, u32[]{:S(2)}) copy-start(s32[31,4]{0,1:T(4,128)} %param.16) | copy-start | bytes 1492
  35.7 0.6 copy-start.4
  36.0 0.6 copy-start.7
  56.4 5.5 %copy-start.3 = (f32[31,32,64]{2,1,0:T(8,128)S(1)}, f32[31,32,64]{2,1,0:T(8,128)}, u32[]{:S(2)}) copy-start(f32[31,32,64]{2,1,0:T(8,128)} %convolution_bitcast_fusion) | copy-start | bytes 761860
  56.4 5.7 %copy-start.5 = (bf16[2,2,64,64]{3,2,1,0:T(8,128)(2,1)S(1)}, bf16[2,2,64,64]{3,2,1,0:T(8,128)(2,1)}, u32[]{:S(2)}) copy-start(bf16[2,2,64,64]{3,2,1,0:T(8,128)(2,1)} %copy-done.4) | copy-start | bytes 98308
  56.4 5.7 %copy-start.8 = (bf16[2,64,64]{2,1,0:T(8,128)(2,1)S(1)}, bf16[2,64,64]{2,1,0:T(8,128)(2,1)}, u32[]{:S(2)}) copy-start(bf16[2,64,64]{2,1,0:T(8,128)(2,1)} %copy-done.7) | copy-start | bytes 49156
  61.8 1.2 %copy-start.2 = (s32[4096]{0:T(1024)S(1)}, s32[4096]{0:T(1024)}, u32[]{:S(2)}) copy-start(s32[4096]{0:T(1024)} %param.12) | copy-start | bytes 49156
